TPU v7x, 128 devices: a whole 4x4x4 slice. The times are simulated.
128 devices in a mesh: seg: 4 (over y), tm: 32 (over z, x, core).
Axes of the slice: x: 4, y: 4, z: 4, core: 2. Of those that a mesh axis runs over, the one named last changes fastest.
Arguments:
- samples: bfloat16 [32, 32768], P('seg', 'tm'), may hold values from -6 to 6
- antenna: bfloat16 [32, 2, 256, 32768], P('seg', None, None, 'tm'), may hold values from -60 to 60
- sky_map: int32 [4096, 32], P(None, 'seg'), may hold values from 0 to 255
- shift_map: int32 [4096, 32], P(None, 'seg'), may hold values from 0 to 7
- owners: int32 [32, 256], P('tm'), may hold values from -1 to 4095, as said below
Outputs:
- fine_stat: float32 [32, 256, 512], P('tm', None, 'seg')
Inputs may be any that keep to these rules, and one draw needn't show every extreme that they name: `owners`: every fine template appears exactly once over all lists; each list holds its templates in its first slots and -1 after them; some list is full with 256 templates.
All inputs are finite; a program needn't handle non-finite values.
Results may differ from a plain program's by a relative error of at most 0.0061.
Values may be sent and summed in bfloat16 or wider, within the bound.
A program may use at most 128 MiB of HBM per device.

v0:
```python
import functools

import jax
import jax.numpy as jnp
import numpy as np
from jax import lax
from jax.experimental import pallas as pl
from jax.experimental.pallas import tpu as pltpu
from jax.sharding import PartitionSpec as P

SAMPLES = 32768
BINS = 512
QUARTERS = 8
HALF_WIDTH = 8
RANK = 60
LANES = 64
WINDOW = 128
BLOCKS = BINS // WINDOW
SIDE = 4
PARTS = 2
MESH = pl.DeviceIdType.MESH

epsilon = 1e-06


def time_basis(span):
    half_band = BINS / SAMPLES
    at = np.arange(span, dtype=np.float64)
    diagonal = ((span - 1 - 2 * at) / 2) ** 2 * np.cos(2 * np.pi * half_band)
    beside = at[1:] * (span - at[1:]) / 2
    matrix = np.diag(diagonal) + np.diag(beside, 1) + np.diag(beside, -1)
    vectors = np.linalg.eigh(matrix)[1][:, ::-1][:, :RANK]
    largest = vectors[np.argmax(np.abs(vectors) > 0.02, axis=0), np.arange(RANK)]
    return vectors * np.where(largest < 0, -1.0, 1.0)


@functools.cache
def factor_tables(span):
    basis = time_basis(span)
    times = np.arange(SAMPLES).reshape(-1, span)
    bins = np.arange(BINS)
    angle = (times[:, :, None] * bins[None, None, :] % SAMPLES) * (2 * np.pi / SAMPLES)
    table = np.concatenate([np.cos(angle), np.sin(angle)], axis=2)
    expansion = np.einsum("tr,dtk->drk", basis, table, optimize=True)
    return basis, expansion


def projection_table(span):
    basis, _ = factor_tables(span)
    high = basis.astype(jnp.bfloat16)
    low = (basis - high.astype(np.float64)).astype(jnp.bfloat16)
    table = np.zeros((2, span, 4, LANES), jnp.bfloat16)
    for a in range(2):
        table[a, :, a, :RANK] = high
        table[a, :, 2 + a, :RANK] = low
    return table.reshape(2 * span, 4 * LANES)


def expansion_table(span):
    _, expansion = factor_tables(span)
    table = np.zeros((expansion.shape[0], LANES, 2 * BINS), jnp.bfloat16)
    table[:, :RANK] = expansion
    return table.reshape(-1, 2 * BINS)


def edge_owner(lane):
    return (lane + 8) // 16 % 8


def sinc_table():
    edge = np.arange(WINDOW) % 16
    edge = np.where(edge < 8, WINDOW + edge, edge - 16)
    source = np.concatenate([np.arange(WINDOW), edge])[None, :, None].astype(np.float64)
    offsets = ((np.arange(QUARTERS) - QUARTERS // 2) * 0.25)[:, None, None]
    target = np.arange(WINDOW)[None, None, :]
    spacing = target + offsets - source
    taper = np.where(np.abs(spacing) < HALF_WIDTH, np.sinc(spacing / HALF_WIDTH), 0.0)
    return (np.sinc(spacing) * taper).astype(jnp.bfloat16).reshape(QUARTERS * 2 * WINDOW, WINDOW)


def kernel(
    samples, owners_hbm, sky_hbm, shift_hbm, antenna, project_hbm, expand_hbm, sinc_hbm, out,
    owners, sky_map, shift_map, ant, project, expand, sinc, weighted, squares, csend, crecv, lhs, cg, onehots, quarters, rows, summed,
    osend, orecv, in_sem, a_send, a_recv, g_send, g_recv, o_send, o_recv,
):
    seg_local, _, sky_count, span = ant.shape
    peers = crecv.shape[1]
    each = crecv.shape[2]
    y = lax.axis_index("seg")
    me = lax.axis_index("tm")
    core = lax.rem(me, 2)
    chip = me // 2
    z = chip // SIDE
    x = lax.rem(chip, SIDE)
    f32, bf16 = jnp.float32, jnp.bfloat16

    load_project = pltpu.make_async_copy(project_hbm, project, in_sem.at[0])
    load_antenna = [pltpu.make_async_copy(antenna.at[s], ant.at[s], in_sem.at[1 + s]) for s in range(seg_local)]
    load_owners = pltpu.make_async_copy(owners_hbm, owners, in_sem.at[seg_local + 5])
    load_sky = pltpu.make_async_copy(sky_hbm, sky_map, in_sem.at[seg_local + 1])
    load_shift = pltpu.make_async_copy(shift_hbm, shift_map, in_sem.at[seg_local + 2])
    load_expand = pltpu.make_async_copy(expand_hbm, expand, in_sem.at[seg_local + 3])
    load_sinc = pltpu.make_async_copy(sinc_hbm, sinc, in_sem.at[seg_local + 4])
    load_project.start()
    for load in load_antenna:
        load.start()

    barrier = pltpu.get_barrier_semaphore()

    def greet(i, carry):
        pl.semaphore_signal(barrier, inc=1, device_id=(y, lax.rem(me + i, peers)), device_id_type=MESH)
        return carry

    lax.fori_loop(1, peers, greet, 0)
    for i in range(1, 4):
        pl.semaphore_signal(barrier, inc=1, device_id=(lax.rem(y + i, 4), me), device_id_type=MESH)

    def coef_start(i, part):
        peer = lax.rem(me + 11 * i, peers)
        pltpu.make_async_remote_copy(
            src_ref=csend.at[part, lax.rem(peer, 2), peer // 2],
            dst_ref=crecv.at[part, me],
            send_sem=a_send.at[part],
            recv_sem=a_recv.at[part],
            device_id=(y, peer),
            device_id_type=MESH,
        ).start()
        return part

    load_project.wait()
    series = samples[...].astype(f32)
    chunk = 32
    lane = lax.broadcasted_iota(jnp.int32, (chunk, 128), 1)
    first = (lane == RANK) | (lane == RANK + 1)
    second = (lane == LANES + RANK) | (lane == LANES + RANK + 1)
    wide_lane = lax.broadcasted_iota(jnp.int32, (2 * sky_count, 128), 1)
    low_lane = (wide_lane == RANK + 1) | (wide_lane == LANES + RANK + 1)
    for j in range(seg_local // 2):
        slot = j % 2
        for c in range(2):
            s = 2 * j + c
            load_antenna[s].wait()
            if s == seg_local - 1:
                for load in (load_owners, load_sky, load_shift, load_expand, load_sinc):
                    load.start()
            scale = series[s : s + 1].astype(bf16)
            for r in range(0, sky_count, chunk):
                at = c * sky_count + r
                norms = []
                for a in range(2):
                    block = ant[s, a, r : r + chunk, :]
                    weighted[slot, at : at + chunk, a * span : (a + 1) * span] = block * scale
                    block = block.astype(f32)
                    norms.append(jnp.sum(block * block, axis=1, keepdims=True))
                squares[slot, at : at + chunk, :] = jnp.where(first, norms[0], jnp.where(second, norms[1], 0.0))
        coefs = jnp.dot(weighted[slot], project[...], preferred_element_type=f32)
        coefs = coefs[:, :128] + coefs[:, 128:] + squares[slot]
        coefs = jnp.where(low_lane, coefs - coefs.astype(bf16).astype(f32), coefs).astype(bf16)
        for c in range(2):
            csend[j // each, c, :, j % each] = coefs[c * sky_count : (c + 1) * sky_count].reshape(sky_count // 16, 16, 128)
        if j % each == each - 1:
            if j == each - 1:
                pl.semaphore_wait(barrier, peers - 1 + 3)
            part = j // each
            lax.fori_loop(1, peers, coef_start, part)
            crecv[part, me] = csend[part, core, chip]

    load_owners.wait()
    load_sky.wait()
    load_shift.wait()
    ids = owners[...]
    templates = sky_map.shape[1]
    maps = jnp.concatenate(
        [sky_map[...].astype(f32), shift_map[...].astype(f32), jnp.ones((16, templates), f32)], axis=0
    ).astype(bf16)
    slots = ids.shape[1]
    step = 512
    found = jnp.zeros((32, slots), f32)
    for t in range(0, templates, step):
        hit = (lax.broadcasted_iota(jnp.int32, (step, slots), 0) + t == ids).astype(f32).astype(bf16)
        found = found + jnp.dot(maps[:, t : t + step], hit, preferred_element_type=f32)
    diagonal = lax.broadcasted_iota(jnp.int32, (slots, slots), 0) == lax.broadcasted_iota(jnp.int32, (slots, slots), 1)
    found = lax.dot_general(
        diagonal.astype(f32).astype(bf16), found.astype(bf16), (((1,), (1,)), ((), ())), preferred_element_type=f32
    )
    dead = found[:, 16:17] < 0.5
    sky_lane = lax.broadcasted_iota(jnp.int32, (slots, sky_count), 1).astype(f32)
    for s in range(seg_local):
        sky = jnp.where(dead, -1.0, found[:, s : s + 1])
        onehots[s] = jnp.where(sky_lane == sky, 1.0, 0.0).astype(bf16)
        quarters[s] = jnp.broadcast_to(found[:, 8 + s : 9 + s], (slots, WINDOW))
    owner = edge_owner(lax.broadcasted_iota(jnp.int32, (slots, WINDOW), 1))
    mixed = quarters[0]
    for s in range(1, seg_local):
        mixed = jnp.where(owner == s, quarters[s], mixed)
    quarters[seg_local] = mixed

    def coef_all(part):
        ref = crecv.at[part, pl.ds(0, peers - 1)]
        return pltpu.make_async_remote_copy(
            src_ref=ref,
            dst_ref=ref,
            send_sem=a_send.at[part],
            recv_sem=a_recv.at[part],
            device_id=(y, me),
            device_id_type=MESH,
        )

    def place(dp, dq):
        zz = lax.rem(z + core * dp + (1 - core) * dq, SIDE)
        xx = lax.rem(x + (1 - core) * dp + core * dq, SIDE)
        return zz * SIDE + xx

    def send(part, block, device, sem):
        ref = cg.at[part * peers + place(*block) * 2 + core]
        pltpu.make_async_remote_copy(
            src_ref=ref,
            dst_ref=ref,
            send_sem=g_send,
            recv_sem=g_recv.at[part, sem],
            device_id=(y, device),
            device_id_type=MESH,
        ).start()

    def arrived(part, count, sem):
        ref = cg.at[pl.ds(0, count)]
        pltpu.make_async_remote_copy(
            src_ref=ref,
            dst_ref=ref,
            send_sem=g_send,
            recv_sem=g_recv.at[part, sem],
            device_id=(y, me),
            device_id_type=MESH,
        ).wait_recv()

    sibling = chip * 2 + 1 - core

    def spread(part, dp):
        for dq in range(1, SIDE):
            send(part, (dp, 0), place(0, dq) * 2 + core, SIDE + (SIDE - dp) % SIDE)
        send(part, (dp, 0), sibling, 0)

    points = 16 * each
    lane = lax.broadcasted_iota(jnp.int32, (points, 128), 1)
    near = lane < LANES
    edges = [jnp.zeros((16, WINDOW), f32)] * BLOCKS
    blank = jnp.zeros((points, WINDOW), f32)
    norm_lane = (lax.rem(lane, LANES) == RANK) | (lax.rem(lane, LANES) == RANK + 1)
    for part in range(PARTS):
        coef_all(part).wait_recv()
        sums = [jnp.zeros((points, 128), f32), jnp.zeros((points, 128), f32)]
        for i in range(peers // 2):
            left = crecv[part, 2 * i].reshape(points, 128).astype(f32)
            right = crecv[part, 2 * i + 1].reshape(points, 128).astype(f32)
            turned = pltpu.roll(jnp.where(near, right, left), LANES, 1)
            pair = [jnp.where(near, left, turned), jnp.where(near, turned, right)]
            for a in range(2):
                lhs[part, a * points : (a + 1) * points, i * 128 : (i + 1) * 128] = pair[a].astype(bf16)
                sums[a] = sums[a] + pair[a]
        if part == 0:
            load_expand.wait()
        demod = jnp.dot(lhs[part], expand[...], preferred_element_type=f32)
        powers = demod[:, :BINS] * demod[:, :BINS] + demod[:, BINS:] * demod[:, BINS:]
        fstat = jnp.zeros((points, BINS), f32)
        for a in range(2):
            norm = jnp.sum(jnp.where(norm_lane, sums[a], 0.0), axis=1, keepdims=True)
            fstat = fstat + powers[a * points : (a + 1) * points] / (norm / SAMPLES + epsilon)
        fstat = fstat / SAMPLES
        coarse = (fstat - jnp.mean(fstat, axis=1, keepdims=True)).astype(bf16)
        tiles = [coarse[:, b * WINDOW : (b + 1) * WINDOW] for b in range(BLOCKS)]
        wide = [blank] + [tile.astype(f32) for tile in tiles] + [blank]
        for b in range(BLOCKS):
            turn = lax.rem(b + 2 * BLOCKS - 1 - y, BLOCKS)
            cg[turn * peers + me, part * points : (part + 1) * points, :] = tiles[b]
            edge = jnp.where(lane < 8, wide[b + 2], jnp.where(lane >= WINDOW - 8, wide[b], 0.0))
            for j in range(each):
                shift = 16 * (2 * (part * each + j) + core)
                edges[b] = edges[b] + pltpu.roll(edge[16 * j : 16 * (j + 1)], shift, 1)
            if part == PARTS - 1:
                cg[turn * peers + me, PARTS * points :, :] = edges[b].astype(bf16)
    for turn in range(BLOCKS):
        for dp in range(1, SIDE):
            send(turn, (0, 0), place(dp, 0) * 2 + core, dp)
    for turn in range(BLOCKS):
        spread(turn, 0)

    chunk = 16

    def group(i, carry):
        at = pl.multiple_of(i * chunk, chunk)
        row = [rows[s, pl.ds(at, chunk), :].astype(f32) for s in range(seg_local + 1)]
        quarter = [quarters[s, pl.ds(at, chunk), :] for s in range(seg_local + 1)]
        for q in range(QUARTERS):
            total = jnp.zeros((chunk, WINDOW), f32)
            for s in range(seg_local):
                total = total + jnp.where(quarter[s] == q, row[s], 0.0)
            edge = jnp.where(quarter[seg_local] == q, row[seg_local], 0.0)
            summed[pl.ds(at, chunk), 2 * q * WINDOW : (2 * q + 1) * WINDOW] = total.astype(bf16)
            summed[pl.ds(at, chunk), (2 * q + 1) * WINDOW : (2 * q + 2) * WINDOW] = edge.astype(bf16)
        return carry

    def from_first(turn):
        for dp in range(1, SIDE):
            arrived(turn, 1, SIDE - dp)
            spread(turn, dp)

    def from_second(turn):
        for dp in range(SIDE):
            arrived(turn, SIDE - 1, SIDE + (SIDE - dp) % SIDE)
            for dq in range(1, SIDE):
                send(turn, (dp, dq), sibling, 0)

    def block_sum(turn):
        arrived(turn, peers // 2, 0)
        base = turn * peers
        edge = [cg[base + i, seg_local * 8 :] + cg[base + i + 1, seg_local * 8 :] for i in range(0, peers, 2)]
        edge = jnp.concatenate(edge, axis=0)
        mixed = jnp.zeros((slots, WINDOW), f32)
        for s in range(seg_local):
            at = s // 2 * 16
            main = jnp.concatenate([cg[base + i, at : at + 16] for i in range(s % 2, peers, 2)], axis=0)
            picked = jnp.dot(onehots[s], jnp.concatenate([main, edge], axis=1), preferred_element_type=f32)
            rows[s] = picked[:, :WINDOW].astype(bf16)
            mixed = jnp.where(owner == s, picked[:, WINDOW:], mixed)
        rows[seg_local] = mixed.astype(bf16)
        lax.fori_loop(0, slots // chunk, group, 0, unroll=16)
        if turn == 0:
            load_sinc.wait()
        block = jnp.dot(summed[...], sinc[...], preferred_element_type=f32)
        if turn == BLOCKS - 1:
            return block
        osend[turn] = block.astype(bf16)
        pltpu.make_async_remote_copy(
            src_ref=osend.at[turn],
            dst_ref=orecv.at[y],
            send_sem=o_send,
            recv_sem=o_recv,
            device_id=(lax.rem(y + 1 + turn, BLOCKS), me),
            device_id_type=MESH,
        ).start()

    for turn in range(BLOCKS):
        from_first(turn)
    from_second(0)
    for turn in range(1, BLOCKS):
        from_second(turn)
        block_sum(turn - 1)
    total = block_sum(BLOCKS - 1)
    three = orecv.at[pl.ds(0, BLOCKS - 1)]
    part_all = pltpu.make_async_remote_copy(
        src_ref=three, dst_ref=three, send_sem=o_send, recv_sem=o_recv, device_id=(y, me), device_id_type=MESH
    )
    part_all.wait_recv()
    for i in range(1, BLOCKS):
        total = total + orecv[lax.rem(y + i, BLOCKS)].astype(f32)
    out[...] = total

    for part in range(PARTS):
        coef_all(part).wait_send()
    ref = cg.at[pl.ds(0, BLOCKS * (peers - 1))]
    pltpu.make_async_remote_copy(
        src_ref=ref, dst_ref=ref, send_sem=g_send, recv_sem=g_recv.at[0, 0], device_id=(y, me), device_id_type=MESH
    ).wait_send()
    part_all.wait_send()


def body(samples, antenna, sky_map, shift_map, owners):
    seg_local, span = samples.shape
    sky_count = antenna.shape[2]
    slots = owners.shape[1]
    peers = SAMPLES // span
    each = seg_local // 2 // PARTS
    bf16, f32 = jnp.bfloat16, jnp.float32
    vmem = pl.BlockSpec(memory_space=pltpu.VMEM)
    hbm = pl.BlockSpec(memory_space=pltpu.HBM)
    dma = pltpu.SemaphoreType.DMA
    result = pl.pallas_call(
        kernel,
        out_shape=jax.ShapeDtypeStruct((slots, BINS // 4), f32),
        in_specs=[vmem] + [hbm] * 7,
        out_specs=vmem,
        scratch_shapes=[
            pltpu.VMEM(owners.shape, jnp.int32),
            pltpu.VMEM(sky_map.shape[::-1], jnp.int32),
            pltpu.VMEM(sky_map.shape[::-1], jnp.int32),
            pltpu.VMEM((seg_local, 2, sky_count, span), bf16),
            pltpu.VMEM((2 * span, 4 * LANES), bf16),
            pltpu.VMEM((peers * LANES, 2 * BINS), bf16),
            pltpu.VMEM((QUARTERS * 2 * WINDOW, WINDOW), bf16),
            pltpu.VMEM((2, 2 * sky_count, 2 * span), bf16),
            pltpu.VMEM((2, 2 * sky_count, 128), f32),
            pltpu.VMEM((PARTS, 2, peers // 2, each, 16, 128), bf16),
            pltpu.VMEM((PARTS, peers, each, 16, 128), bf16),
            pltpu.VMEM((PARTS, 32 * each, peers * LANES), bf16),
            pltpu.VMEM((BLOCKS * peers, seg_local * 8 + 16, WINDOW), bf16),
            pltpu.VMEM((seg_local, slots, sky_count), bf16),
            pltpu.VMEM((seg_local + 1, slots, WINDOW), f32),
            pltpu.VMEM((seg_local + 1, slots, WINDOW), bf16),
            pltpu.VMEM((slots, QUARTERS * 2 * WINDOW), bf16),
            pltpu.VMEM((BLOCKS, slots, WINDOW), bf16),
            pltpu.VMEM((BLOCKS, slots, WINDOW), bf16),
            dma((seg_local + 6,)),
            dma((PARTS,)),
            dma((PARTS,)),
            dma,
            dma((BLOCKS, 2 * SIDE)),
            dma,
            dma,
        ],
        compiler_params=pltpu.CompilerParams(
            collective_id=0, has_side_effects=True, vmem_limit_bytes=56 * 1024 * 1024
        ),
    )(
        samples,
        owners,
        sky_map.T,
        shift_map.T,
        antenna,
        jnp.asarray(projection_table(span)),
        jnp.asarray(expansion_table(span)),
        jnp.asarray(sinc_table()),
    )
    return result[None]


def solution(mesh):
    in_specs = (
        P("seg", "tm"),
        P("seg", None, None, "tm"),
        P(None, "seg"),
        P(None, "seg"),
        P("tm", None),
    )
    out_specs = P("tm", None, "seg")
    return jax.shard_map(body, mesh=mesh, in_specs=in_specs, out_specs=out_specs, check_vma=False)
```

profile of v0, /device:TPU:9, one launch (start us, length us, event | category | flops | bytes accessed | tf_op | source)
XLA Modules:
  0.0 41.0 jit_solution(15279363482197274032)
XLA Ops:
  0.0 39.5 %shard_map.82 = f32[256,128]{1,0:T(8,128)} custom-call(bf16[8,1024]{1,0:T(8,128)(2,1)} %samples.1, s32[1,256]{1,0:T(1,128)} %owners_hbm.1, s32[8,4096]{1,0:T(8,128)} %bitcast.4, s32[8,4096]{1,0:T(8,128)} %bitcast.5, bf16[8,2,256,1024]{3,2,1,0:T(8,128)(2,1)} %antenna.1, bf16[2048,256]{1,0:T(8,128)(2,1)} %constant.6.clone.project_hbm, ...), custom_call_target="tpu_custom_call" | custom-call | tf_op jit(solution)/shard_map/pallas_call | solution.py:377
  39.5 1.6 %copy.10 = f32[1,256,128]{2,1,0:T(8,128)} copy(f32[1,256,128]{2,1,0:T(8,128)} %bitcast.3) | data formatting | bytes 262144
where the time goes:
time: 41.2 us; the launch traced here: 41 us
  Pallas kernels  39.5 us (96%)
  local copies, waits for them, and re-layouts  1.57 us (4%)
    pallas_call x1, Pallas kernels, body(): pl.pallas_call(kernel, out_shape=jax.ShapeDtypeStruct((slots, BINS // 4),...  39.5 us
    unnamed x1, local copies, waits for them, and re-layouts  1.57 us

commit v1 on v0

--- a/solution.py
+++ b/solution.py
@@ -48,12 +48,10 @@
 def projection_table(span):
     basis, _ = factor_tables(span)
     high = basis.astype(jnp.bfloat16)
-    low = (basis - high.astype(np.float64)).astype(jnp.bfloat16)
-    table = np.zeros((2, span, 4, LANES), jnp.bfloat16)
-    for a in range(2):
-        table[a, :, a, :RANK] = high
-        table[a, :, 2 + a, :RANK] = low
-    return table.reshape(2 * span, 4 * LANES)
+    table = np.zeros((span, 2, LANES), jnp.bfloat16)
+    table[:, 0, :RANK] = high
+    table[:, 1, :RANK] = (basis - high.astype(np.float64)).astype(jnp.bfloat16)
+    return table.reshape(span, 2 * LANES)
 
 
 def expansion_table(span):
@@ -80,7 +78,7 @@
 
 def kernel(
     samples, owners_hbm, sky_hbm, shift_hbm, antenna, project_hbm, expand_hbm, sinc_hbm, out,
-    owners, sky_map, shift_map, ant, project, expand, sinc, weighted, squares, csend, crecv, lhs, cg, onehots, quarters, rows, summed,
+    owners, sky_map, shift_map, ant, basis, project, expand, sinc, weighted, squares, csend, crecv, lhs, cg, onehots, quarters, rows, summed,
     osend, orecv, in_sem, a_send, a_recv, g_send, g_recv, o_send, o_recv,
 ):
     seg_local, _, sky_count, span = ant.shape
@@ -94,7 +92,7 @@
     x = lax.rem(chip, SIDE)
     f32, bf16 = jnp.float32, jnp.bfloat16
 
-    load_project = pltpu.make_async_copy(project_hbm, project, in_sem.at[0])
+    load_project = pltpu.make_async_copy(project_hbm, basis, in_sem.at[0])
     load_antenna = [pltpu.make_async_copy(antenna.at[s], ant.at[s], in_sem.at[1 + s]) for s in range(seg_local)]
     load_owners = pltpu.make_async_copy(owners_hbm, owners, in_sem.at[seg_local + 5])
     load_sky = pltpu.make_async_copy(sky_hbm, sky_map, in_sem.at[seg_local + 1])
@@ -128,6 +126,13 @@
         return part
 
     load_project.wait()
+    straight = basis[...].astype(f32)
+    turned = pltpu.roll(straight, LANES, 1)
+    front = lax.broadcasted_iota(jnp.int32, straight.shape, 1) < LANES
+    project[:span, :128] = jnp.where(front, straight, 0.0).astype(bf16)
+    project[:span, 128:] = jnp.where(front, turned, 0.0).astype(bf16)
+    project[span:, :128] = jnp.where(front, 0.0, turned).astype(bf16)
+    project[span:, 128:] = jnp.where(front, 0.0, straight).astype(bf16)
     series = samples[...].astype(f32)
     chunk = 32
     lane = lax.broadcasted_iota(jnp.int32, (chunk, 128), 1)
@@ -384,6 +389,7 @@
             pltpu.VMEM(sky_map.shape[::-1], jnp.int32),
             pltpu.VMEM(sky_map.shape[::-1], jnp.int32),
             pltpu.VMEM((seg_local, 2, sky_count, span), bf16),
+            pltpu.VMEM((span, 2 * LANES), bf16),
             pltpu.VMEM((2 * span, 4 * LANES), bf16),
             pltpu.VMEM((peers * LANES, 2 * BINS), bf16),
             pltpu.VMEM((QUARTERS * 2 * WINDOW, WINDOW), bf16),

time: 41.2 us -> 41 us (level)
  no operation moved by 1% of the time
where the time goes in v1:
time: 41 us; the launch traced here: 40.8 us
  Pallas kernels  39.2 us (96%)
  local copies, waits for them, and re-layouts  1.57 us (4%)
    pallas_call x1, Pallas kernels, body(): pl.pallas_call(kernel, out_shape=jax.ShapeDtypeStruct((slots, BINS // 4),...  39.2 us
    unnamed x1, local copies, waits for them, and re-layouts  1.57 us

profile of v1, /device:TPU:9, one launch (start us, length us, event | category | flops | bytes accessed | tf_op | source)
XLA Modules:
  0.0 40.8 jit_solution(11100323732631274268)
XLA Ops:
  0.0 39.2 %shard_map.82 = f32[256,128]{1,0:T(8,128)} custom-call(bf16[8,1024]{1,0:T(8,128)(2,1)} %samples.1, s32[1,256]{1,0:T(1,128)} %owners_hbm.1, s32[8,4096]{1,0:T(8,128)} %bitcast.4, s32[8,4096]{1,0:T(8,128)} %bitcast.5, bf16[8,2,256,1024]{3,2,1,0:T(8,128)(2,1)} %antenna.1, bf16[1024,128]{1,0:T(8,128)(2,1)} %constant.6.clone.project_hbm, ...), custom_call_target="tpu_custom_call" | custom-call | tf_op jit(solution)/shard_map/pallas_call | solution.py:382
  39.2 1.6 %copy.10 = f32[1,256,128]{2,1,0:T(8,128)} copy(f32[1,256,128]{2,1,0:T(8,128)} %bitcast.3) | data formatting | bytes 262144
